TPU v7x, 128 devices: a whole 4x4x4 slice. The times are simulated.
128 devices in a mesh: dp: 16 (over y, x_lo, core), seq: 8 (over x_hi, z).
Axes of the slice: x: 4 (x_hi: 2, x_lo: 2; x = x_hi * 2 + x_lo), y: 4, z: 4, core: 2. Of those that a mesh axis runs over, the one named last changes fastest.
Arguments:
- tokens: bfloat16 [16384, 1280], P(('dp', 'seq')), may hold values from -24 to 24
- teacher: bfloat16 [16384, 1280], P(('dp', 'seq')), may hold values from -20 to 20
- prefix: int32 [16], replicated, may hold values from 1 to 1024
- routes: int32 [16384, 2], P(('dp', 'seq')), may hold values from 0 to 2, all different within a row
- attn_gain: bfloat16 [1280], P(('dp', 'seq')), may hold values from 0.099609375 to 1.8984375
- w_qkv: bfloat16 [1280, 3840], P(('dp', 'seq')), may hold values from -0.15625 to 0.15625
- w_out: bfloat16 [1280, 1280], P(('dp', 'seq')), may hold values from -2 to 2
- router_w: bfloat16 [1280, 3], P(('dp', 'seq')), may hold values from -0.078125 to 0.078125
- ffn_gain: bfloat16 [1280], P(('dp', 'seq')), may hold values from 0.099609375 to 1.8984375
- w_gate_up: bfloat16 [1280, 4, 2, 896], P('dp', None, None, 'seq'), may hold values from -0.15625 to 0.15625
- w_down: bfloat16 [1280, 4, 896], P('dp', None, 'seq'), may hold values from -0.1875 to 0.1875
Outputs:
- activations: bfloat16 [16384, 1280], P(('dp', 'seq'))
- loss: float32 [], replicated
- d_tokens: float32 [16384, 1280], P(('dp', 'seq'))
- d_attn_gain: float32 [1280], P(('dp', 'seq'))
- d_w_qkv: float32 [1280, 3840], P(('dp', 'seq'))
- d_w_out: float32 [1280, 1280], P(('dp', 'seq'))
- d_router_w: float32 [1280, 3], P(('dp', 'seq'))
- d_ffn_gain: float32 [1280], P(('dp', 'seq'))
- d_w_gate_up: float32 [1280, 4, 2, 896], P('dp', None, None, 'seq')
- d_w_down: float32 [1280, 4, 896], P('dp', None, 'seq')
Inputs may be any that keep to these rules, and one draw needn't show every extreme that they name: `routes`: each token's 2 routed experts are different.
All inputs are finite; a program needn't handle non-finite values.
Results may differ from a plain program's by a relative error of at most 0.017.
Values may be sent and summed in bfloat16 or wider, within the bound.
No kernel may reach another device: no remote copies, remote signals or barrier semaphores. Data moves between devices by JAX's collectives and lax.ppermute only.
A program may use at most 192 MiB of HBM per device.

v0:
```python
import functools

import jax
import jax.numpy as jnp
import numpy as np
from jax import lax
from jax.experimental import pallas as pl
from jax.experimental.pallas import tpu as pltpu
from jax.sharding import Mesh, PartitionSpec as P

D = 1280
HD = 128
HEADS = 10
SLOTS = 2
GROUPS = 5
HW = SLOTS * HD
QKV = 3 * HW
EXT = 128
WQ = QKV + EXT
WA = WQ + HW
ROWS = 128
SEQ = 1024
UNITS = 112
GU = 4 * 2 * 128
DN = 4 * 128
WM = GU + DN
PART = 80
SPLIT_A = 640
SPLIT_M = 768
norm_eps = 1e-06
masked_score = -1e30
rope_base = 10000.0
SCALE = HD ** (-0.5)
LOG2E = float(np.log2(np.e))
SLOT = 3 * HD
F32 = jnp.float32
BF16 = jnp.bfloat16
MIB = 1024 * 1024
LIM = (52, 12, 10, 10, 12, 50, 10, 50)

NT = (((1,), (1,)), ((), ()))
TN = (((0,), (0,)), ((), ()))


def dot(a, b):
    return jnp.dot(a, b, preferred_element_type=F32)


def dot_nt(a, b):
    return lax.dot_general(a, b, NT, preferred_element_type=F32)


def dot_tn(a, b):
    return lax.dot_general(a, b, TN, preferred_element_type=F32)


def rows_of(start, count=ROWS):
    return pl.ds(pl.multiple_of(start, ROWS), count)


def half_turn(u):
    return pltpu.roll(u, HD // 2, 1)


def natural_rows(placed, out, first):
    half = PART // 2
    columns = slice(first, first + out.shape[1])
    for p in range(8):
        at = (p // 2 * 4 + p % 2) * PART
        low = placed[at : at + PART, columns].astype(F32)
        high = placed[at + 2 * PART : at + 3 * PART, columns].astype(F32)
        for i in range(2):
            cut = slice(i * half, (i + 1) * half)
            to = (2 * p + i) * PART
            out[to : to + PART, :] = jnp.concatenate([low[cut], high[cut]], axis=0).astype(BF16)


def place_kernel(info, *refs):
    x, chosen = refs[8:]
    for i in range(8):
        at = rows_of(info[i] * ROWS)
        x[at, :] = refs[i][:, :D]
        chosen[at, :] = refs[i][:, D:]


def masked(s, step, prefix):
    first = step * 256
    rest = s[first:]
    key = lax.broadcasted_iota(jnp.int32, rest.shape, 0)
    query = lax.broadcasted_iota(jnp.int32, rest.shape, 1)
    rest = jnp.where(key < jnp.maximum(query + 1, prefix - first), rest, masked_score)
    return rest if step == 0 else jnp.concatenate([s[:first], rest], axis=0)


def attn_fwd_kernel(info, w_far, x, cos, sin, *refs):
    saved = refs[:7]
    a, b, wext, lse, ext = refs[7:12]
    w, h1, q, k, v, mixed, wo, wp, vt, part, sems = refs[12:]
    held = [w, h1, q, k, v, mixed, wo]

    def keep(i):
        return pltpu.make_async_copy(held[i], saved[i], sems.at[i])

    load = pltpu.make_async_copy(w_far, wp, sems.at[7])
    load.start()
    load.wait()
    natural_rows(wp, w, 0)
    natural_rows(wp, wo, WQ)
    keep(0).start()
    keep(6).start()
    wext[...] = w[:, QKV:]
    ext_t = w[:, QKV:].astype(F32).T
    ext[...] = ext_t
    gain = ext_t[0:1, :]

    @pl.loop(0, 4)
    def _(step):
        at = rows_of(step * 256, 256)
        blk = x[at, :].astype(F32)
        r = lax.rsqrt(jnp.mean(blk * blk, axis=1, keepdims=True) + norm_eps)
        h = (blk * r * gain).astype(BF16)
        h1[at, :] = h
        full = dot(h, w[:, :QKV])
        c, s = cos[at, :], sin[at, :]
        for j in range(SLOTS):
            col = slice(j * HD, (j + 1) * HD)
            uq, uk, uv = (
                full[:, j * SLOT + i * HD : j * SLOT + (i + 1) * HD] for i in range(3)
            )
            q[at, col] = (uq * c + half_turn(uq) * s).astype(BF16)
            k[at, col] = (uk * c + half_turn(uk) * s).astype(BF16)
            v[at, col] = uv.astype(BF16)
            vt[col, at] = uv.T.astype(BF16)

    for i in range(1, 5):
        keep(i).start()
    lse[...] = jnp.zeros_like(lse)
    for j in range(SLOTS):
        col = slice(j * HD, (j + 1) * HD)
        for step in range(4):
            at = slice(step * 256, (step + 1) * 256)
            s = masked(dot_nt(k[:, col], q[at, col]), step, info[16])
            top = jnp.max(s, axis=0, keepdims=True)
            e = jnp.exp2((s - top) * (SCALE * LOG2E))
            total = jnp.sum(e, axis=0, keepdims=True)
            mix = dot(vt[col, :], e.astype(BF16)) * (1.0 / total)
            mixed[at, col] = mix.T.astype(BF16)
            lse[j : j + 1, at] = top * (SCALE * LOG2E) + jnp.log2(total)

    keep(5).start()

    @pl.loop(0, 4)
    def _(step):
        at = rows_of(step * 256, 256)
        part[at, :] = dot_nt(mixed[at, :], wo[...]).astype(BF16)

    give_blocks(info, part, a, b)
    for i in range(7):
        keep(i).wait()


def give_blocks(info, part, a, b):
    for i in range(4):
        out = slice(i * ROWS, (i + 1) * ROWS)
        a[out, :] = part[rows_of(info[8 + i] * ROWS), :]
        b[out, :] = part[rows_of(info[12 + i] * ROWS), :]


def moe_fwd_kernel(info, *refs):
    hs = refs[:8]
    wm, wext, chosen = refs[8:11]
    a, b, h2, gu, z, comb = refs[11:17]
    (part,) = refs[17:]
    for i in range(8):
        h2[rows_of(info[i] * ROWS), :] = hs[i][...]

    @pl.loop(0, 4)
    def _(step):
        at = rows_of(step * 256, 256)
        h = h2[at, :]
        logits = dot(h, wext[...])
        lane = lax.broadcasted_iota(jnp.int32, logits.shape, 1)
        live = (lane >= 2) & (lane < 5)
        logits = jnp.where(live, logits, masked_score)
        e = jnp.exp(logits - jnp.max(logits, axis=1, keepdims=True))
        gates = e / jnp.sum(e, axis=1, keepdims=True)
        cb = gates * chosen[at, :].astype(F32)
        comb[at, :] = cb
        full = dot(h, wm[:, :GU])
        gu[at, :] = full
        for x in range(4):
            gate = full[:, x * 256 : x * 256 + 128]
            up = full[:, x * 256 + 128 : x * 256 + 256]
            act = gate * jax.nn.sigmoid(gate) * up
            if x:
                act = act * cb[:, x + 1 : x + 2]
            z[at, x * 128 : (x + 1) * 128] = act.astype(BF16)
        part[at, :] = dot_nt(z[at, :], wm[:, GU:]).astype(BF16)

    give_blocks(info, part, a, b)


def moe_bwd_kernel(info, *refs):
    ds = refs[:8]
    wm, gu, comb = refs[8:11]
    a, b, dm, dgu = refs[11:15]
    (part,) = refs[15:]
    for i in range(8):
        dm[rows_of(info[i] * ROWS), :] = ds[i][...]

    @pl.loop(0, 4)
    def _(step):
        at = rows_of(step * 256, 256)
        dz = dot(dm[at, :], wm[:, GU:])
        cb = comb[at, :]
        lane = lax.broadcasted_iota(jnp.int32, (256, 128), 1)
        extra = jnp.zeros((256, 128), F32)
        for x in range(4):
            gate = gu[at, x * 256 : x * 256 + 128]
            up = gu[at, x * 256 + 128 : x * 256 + 256]
            sig = jax.nn.sigmoid(gate)
            silu = gate * sig
            dact = dz[:, x * 128 : (x + 1) * 128]
            if x:
                dc = jnp.sum(dact * (silu * up), axis=1, keepdims=True)
                high = dc.astype(BF16).astype(F32)
                extra = jnp.where(lane == x + 1, high, extra)
                extra = jnp.where(lane == x + 4, dc - high, extra)
                dact = dact * cb[:, x + 1 : x + 2]
            dgu[at, x * 256 : x * 256 + 128] = (
                dact * up * sig * (1.0 + gate * (1.0 - sig))
            ).astype(BF16)
            dgu[at, x * 256 + 128 : x * 256 + 256] = (dact * silu).astype(BF16)
        part[at, :D] = dot_nt(dgu[at, :], wm[:, :GU]).astype(BF16)
        part[at, D:] = extra.astype(BF16)

    give_blocks(info, part, a, b)


def moe_grad_kernel(info, *refs):
    h2, dgu, dm, z, saved, rows, sems = refs

    def keep(i):
        cut = slice(i * 640, (i + 1) * 640)
        return pltpu.make_async_copy(rows.at[cut, :], saved.at[cut, :], sems.at[i])

    for i in range(2):
        cut = slice(i * 640, (i + 1) * 640)
        rows[cut, :GU] = dot_tn(h2[:, cut], dgu[...]).astype(BF16)
        rows[cut, GU:] = dot_tn(dm[:, cut], z[...]).astype(BF16)
        keep(i).start()
    for i in range(2):
        keep(i).wait()


def slot_bwd(j, info, k, q, v, dm, mixed, lse, cos, sin, dqkv, kt, dk, dv):
    kt[...] = k[...].astype(F32).T.astype(BF16)
    for step in range(4):
        at = slice(step * 256, (step + 1) * 256)
        qb, dmb = q[at, :], dm[at, :]
        s = masked(dot_nt(k[...], qb), step, info[16])
        p = jnp.exp2(s * (SCALE * LOG2E) - lse[j : j + 1, at])
        more = dot(p.astype(BF16), dmb)
        dv[...] = more if step == 0 else dv[...] + more
        delta = jnp.sum((dmb.astype(F32) * mixed[at, :].astype(F32)).T, axis=0, keepdims=True)
        ds = (p * (dot_nt(v[...], dmb) - delta)).astype(BF16)
        more = dot(ds, qb)
        dk[...] = more if step == 0 else dk[...] + more
        dq = dot(kt[...], ds).T * SCALE
        dqkv[at, :HD] = (dq * cos[at, :] - half_turn(dq) * sin[at, :]).astype(BF16)
    u = dk[...] * SCALE
    dqkv[:, HD : 2 * HD] = (u * cos[...] - half_turn(u) * sin[...]).astype(BF16)
    dqkv[:, 2 * HD :] = dv[...].astype(BF16)


def to_places(full, i, rows):
    half = PART // 2
    for p in range(4):
        for g in range(2):
            top = p * 2 * PART + g * half
            to = i * 640 + (p * 2 + g) * PART
            rows[to : to + PART, :] = jnp.concatenate(
                [full[top : top + half], full[top + PART : top + PART + half]], axis=0
            ).astype(BF16)


def pick_y(info, rows, outs):
    for j in range(4):
        for m in range(4):
            at = pl.ds(pl.multiple_of(info[32 + j * 4 + m], 16), PART)
            outs[j][m * PART : (m + 1) * PART, :] = rows[at, :]


def pick_x(info, rows, outs):
    for j in range(4):
        for m in range(4):
            at = pl.ds(pl.multiple_of(info[32 + j * 4 + m], 16), PART)
            outs[m][j * PART : (j + 1) * PART, :] = rows[at, :]


def head_loads(j, far, near, sems):
    col = slice(j * HD, (j + 1) * HD)
    return [
        pltpu.make_async_copy(a.at[:, col], b, sems.at[i])
        for i, (a, b) in enumerate(zip(far, near))
    ]


def attn_bwd_kernel(info, *refs):
    ds = refs[:8]
    wo_far, k_far, q_far, v_far, mixed_far, h1_far, w_far, cos, sin, lse = refs[8:18]
    outs = refs[18:22]
    dqkv, dm1, gain = refs[22:25]
    k, q, v, wo, mixed, h1, w, da, dm0, kt, dk, dv, rows, sems = refs[25:]
    loads = [
        pltpu.make_async_copy(wo_far, wo, sems.at[3]),
        pltpu.make_async_copy(mixed_far, mixed, sems.at[4]),
        pltpu.make_async_copy(h1_far, h1, sems.at[5]),
        pltpu.make_async_copy(w_far.at[:, :SLOT], w, sems.at[6]),
    ]
    loads[0].start()
    heads = head_loads(0, (k_far, q_far, v_far), (k, q, v), sems)
    for load in heads + loads[1:]:
        load.start()
    for i in range(8):
        da[rows_of(info[i] * ROWS), :] = ds[i][...]
    loads[0].wait()

    @pl.loop(0, 4)
    def _(step):
        at = rows_of(step * 256, 256)
        dmix = dot(da[at, :], wo[...]).astype(BF16)
        dm0[at, :] = dmix[:, :HD]
        dm1[at, :] = dmix[:, HD:]

    for load in heads + loads[1:2]:
        load.wait()
    slot_bwd(0, info, k, q, v, dm0, mixed.at[:, :HD], lse, cos, sin, dqkv, kt, dk, dv)
    for load in loads[2:]:
        load.wait()
    for i in range(2):
        cut = slice(i * 640, (i + 1) * 640)
        dw = dot_tn(h1[:, cut], dqkv[...])
        gain[cut, :] = jnp.sum(dw * w[cut, :].astype(F32), axis=1, keepdims=True)
        do = dot_tn(da[:, cut], mixed[...])
        to_places(jnp.concatenate([dw, do], axis=1), i, rows)
    pick_y(info, rows, outs)


def attn_bwd_second_kernel(info, *refs):
    dm, k_far, q_far, v_far, mixed_far, h1_far, w_far, cos, sin, lse, gain, sums = refs[:12]
    outs = refs[12:16]
    dqkv = refs[16]
    k, q, v, mixed, h1, w, kt, dk, dv, rows, sems = refs[17:]
    loads = [
        pltpu.make_async_copy(h1_far, h1, sems.at[5]),
        pltpu.make_async_copy(w_far.at[:, SLOT:], w, sems.at[6]),
    ]
    heads = head_loads(1, (k_far, q_far, v_far, mixed_far), (k, q, v, mixed), sems)
    for load in heads + loads:
        load.start()
    for load in heads:
        load.wait()
    slot_bwd(1, info, k, q, v, dm, mixed, lse, cos, sin, dqkv, kt, dk, dv)
    for load in loads:
        load.wait()
    for i in range(2):
        cut = slice(i * 640, (i + 1) * 640)
        dw = dot_tn(h1[:, cut], dqkv[...])
        both = gain[cut, :] + jnp.sum(dw * w[cut, :SLOT].astype(F32), axis=1, keepdims=True)
        extra = sums[:, cut].T
        lane = lax.broadcasted_iota(jnp.int32, extra.shape, 1)
        extra = jnp.where(lane == 0, both / w[cut, SLOT : SLOT + 1].astype(F32), extra)
        to_places(jnp.concatenate([dw, extra], axis=1), i, rows)
    pick_x(info, rows, outs)


def attn_in_kernel(info, *refs):
    w, dq0, dq1, a, b, part = refs

    @pl.loop(0, 4)
    def _(step):
        at = rows_of(step * 256, 256)
        both = jnp.concatenate([dq0[at, :], dq1[at, :]], axis=1)
        part[at, :] = dot_nt(both, w[:, :QKV]).astype(BF16)

    give_blocks(info, part, a, b)


def finish_kernel(info, dw, qkv, out, gains, router, loss):
    for g in range(GROUPS):
        for j in range(SLOTS):
            for part in range(3):
                to = part * D + g * HW + j * HD
                at = j * SPLIT_A + part * HD
                qkv[:, to : to + HD] = dw[g, :, at : at + HD].astype(F32)
        out[:, g * HW : (g + 1) * HW] = dw[g, :, SLOT:SPLIT_A].astype(F32)
    last = slice(SPLIT_A + SLOT, WA)
    total = dw[0, :, last].astype(F32)
    for g in range(1, 8):
        total = total + dw[g, :, last].astype(F32)
    router[...] = total[:, 2:5]
    loss[...] = total[0:1, 5:6]
    gains[...] = total.T[0:8, :]


def call(kernel, info, args, outs, scratch, flops, mib, far_in=(), far_out=(), sems=0):
    total = sum(int(np.prod(x.shape)) * x.dtype.itemsize for x in args)
    total += sum(int(np.prod(s)) * jnp.dtype(t).itemsize for s, t in outs)

    def spec(far):
        return pl.BlockSpec(memory_space=pltpu.HBM if far else pltpu.VMEM)

    return pl.pallas_call(
        kernel,
        out_shape=[jax.ShapeDtypeStruct(s, t) for s, t in outs],
        in_specs=[pl.BlockSpec(memory_space=pltpu.SMEM)]
        + [spec(i in far_in) for i in range(len(args))],
        out_specs=[spec(i in far_out) for i in range(len(outs))],
        scratch_shapes=[pltpu.VMEM(s, t) for s, t in scratch]
        + ([pltpu.SemaphoreType.DMA((sems,))] if sems else []),
        compiler_params=pltpu.CompilerParams(vmem_limit_bytes=mib * MIB),
        cost_estimate=pl.CostEstimate(flops=flops, bytes_accessed=total, transcendentals=0),
    )(info, *args)


def exchange(x):
    return lax.ppermute(x, ("c", "xh"), [(0, 0), (1, 2), (2, 1), (3, 3)])


def turn_out(x):
    pairs = [(i * 4 + j * 2 + k, j * 4 + k * 2 + i) for i in (0, 1) for j in (0, 1) for k in (0, 1)]
    return lax.ppermute(x, ("xl", "c", "xh"), pairs)


def turn_home(x):
    pairs = [(j * 4 + k * 2 + i, i * 4 + j * 2 + k) for i in (0, 1) for j in (0, 1) for k in (0, 1)]
    return lax.ppermute(x, ("xl", "c", "xh"), pairs)


def along_z(x, k):
    return lax.ppermute(x, "z", [(i, (i + k) % 4) for i in range(4)])


def along_y(x, k):
    return lax.ppermute(x, "y", [(i, (i + k) % 4) for i in range(4)])


def along_x(x, k):
    place = [0, 2, 1, 3]
    return lax.ppermute(x, ("xl", "xh"), [(place[i], place[(i + k) % 4]) for i in range(4)])


def after(x, *deps):
    return lax.optimization_barrier((x, deps))[0]


def add_parts(parts, move):
    total = parts[0].astype(F32)
    for k in (1, 2, 3):
        total = total + move(parts[k], k).astype(F32)
    return total.astype(BF16)


def to_other_core(x):
    return lax.ppermute(x, "c", [(0, 1), (1, 0)])


def gather_group(x, *deps):
    own = [x] + [along_z(x, k) for k in (1, 2, 3)]
    last = after(own[3], *deps) if deps else own[3]
    return own + [to_other_core(part) for part in own[:3] + [last]]


def scatter_group(a, b):
    got = to_other_core(b)
    s = [
        (a[i * ROWS : (i + 1) * ROWS].astype(F32) + got[i * ROWS : (i + 1) * ROWS].astype(F32))
        for i in range(4)
    ]
    total = s[0]
    for k in (1, 2, 3):
        total = total + along_z(s[k].astype(BF16), k).astype(F32)
    return total


def sum_cores(a, b):
    got = to_other_core(b)
    cuts = [slice(k * ROWS, (k + 1) * ROWS) for k in range(4)]
    return [(a[cut].astype(F32) + got[cut].astype(F32)).astype(BF16) for cut in cuts]


def scatter_home(parts):
    total = 0.0
    for k in range(4):
        pairs = [
            (c * 8 + x * 4 + z, x * 8 + c * 4 + (z + k) % 4)
            for c in range(2)
            for x in range(2)
            for z in range(4)
        ]
        total = total + lax.ppermute(parts[k], ("c", "xh", "z"), pairs).astype(F32)
    return total


PLANE = ("y", "xl", "xh")
RING = ("y", "xh", "xl")


def rope_tables():
    places = jnp.arange(SEQ, dtype=jnp.int32).astype(F32)
    half = HD // 2
    speeds = rope_base ** (-jnp.arange(half, dtype=F32) / half)
    angles = places[:, None] * speeds[None, :]
    c, s = jnp.cos(angles), jnp.sin(angles)
    return jnp.concatenate([c, c], axis=1), jnp.concatenate([-s, s], axis=1)


def on_device(
    tokens, teacher, prefix, routes, attn_gain, w_qkv, w_out, router_w, ffn_gain, w_gate_up, w_down
):
    core, zz = lax.axis_index("c"), lax.axis_index("z")
    near = [core * 4 + (zz + k) % 4 for k in range(4)]
    far = [(1 - core) * 4 + (zz + k) % 4 for k in range(4)]
    back = [0, 3, 2, 1]
    sequence = lax.axis_index(PLANE)
    yy = lax.axis_index("y")
    xx = lax.axis_index("xh") * 2 + lax.axis_index("xl")

    def place(dy, dx):
        y, x = (yy + dy) % 4, (xx + dx) % 4
        return (y * 4 + x % 2 * 2 + x // 2) * PART

    info = jnp.stack(
        [near[i] for i in back]
        + [far[i] for i in back]
        + near
        + far
        + [prefix[sequence]]
        + [jnp.int32(0)] * 15
        + [place(j, m) for j in range(4) for m in range(4)]
    ).astype(jnp.int32)

    lanes = jnp.arange(EXT, dtype=jnp.int32)[None, :]
    chosen = (routes[:, 0:1] + 2 == lanes) | (routes[:, 1:2] + 2 == lanes)
    x_all = exchange(jnp.concatenate([tokens, chosen.astype(BF16)], axis=1))
    small = jnp.concatenate([attn_gain[:, None], ffn_gain[:, None], router_w], axis=1)
    raw = jnp.concatenate([w_qkv, w_out, jnp.pad(small, ((0, 0), (0, EXT - 5)))], axis=1)
    n = raw.shape[0]
    heads = raw[:, : 3 * D].reshape(n, 3, GROUPS, SLOTS, HD).transpose(2, 0, 3, 1, 4)
    outs = raw[:, 3 * D : 4 * D].reshape(n, GROUPS, HW).transpose(1, 0, 2)
    extra = jnp.broadcast_to(raw[None, :, 4 * D :], (8, n, EXT))
    none = ((0, 8 - GROUPS), (0, 0), (0, 0))
    packed = jnp.concatenate(
        [jnp.pad(heads.reshape(GROUPS, n, QKV), none), extra, jnp.pad(outs, none)], axis=2
    )
    packed = lax.all_to_all(packed, ("c", "z"), split_axis=0, concat_axis=0).reshape(8 * n, WA)
    lane_pad = 128 - UNITS
    wm_own = jnp.concatenate(
        [
            jnp.pad(w_gate_up, ((0, 0), (0, 0), (0, 0), (0, lane_pad))).reshape(-1, GU),
            jnp.pad(w_down, ((0, 0), (0, 0), (0, lane_pad))).reshape(-1, DN),
        ],
        axis=1,
    )
    wm_own = turn_out(wm_own)
    w_all = lax.all_gather(packed, RING, axis=0, tiled=True)
    x_seq, chosen_all = call(
        place_kernel,
        info,
        gather_group(x_all),
        [((SEQ, D), BF16), ((SEQ, EXT), BF16)],
        [],
        0,
        6,
    )
    wm = lax.all_gather(after(wm_own, w_all, x_seq), RING, axis=0, tiled=True)
    teach = exchange(teacher)
    cos, sin = rope_tables()

    head = ((SEQ, HW), BF16)
    w, h1, q, k, v, mixed, wo, a, b, wext, lse, ext = call(
        attn_fwd_kernel,
        info,
        [w_all, x_seq, cos, sin],
        [
            ((D, WQ), BF16),
            ((SEQ, D), BF16),
            head,
            head,
            head,
            head,
            ((D, HW), BF16),
            ((512, D), BF16),
            ((512, D), BF16),
            ((D, EXT), BF16),
            ((8, SEQ), F32),
            ((EXT, D), F32),
        ],
        [
            ((D, WQ), BF16),
            ((SEQ, D), BF16),
            head,
            head,
            head,
            head,
            ((D, HW), BF16),
            ((D, WA), BF16),
            ((HW, SEQ), BF16),
            ((SEQ, D), BF16),
        ],
        5_000_000_000,
        LIM[0],
        far_in=(0,),
        far_out=range(7),
        sems=8,
    )
    x = x_all[:, :D].astype(F32)
    x1 = x + scatter_group(a, b)
    r2 = lax.rsqrt(jnp.mean(x1 * x1, axis=1, keepdims=True) + norm_eps)
    n2 = x1 * r2
    gain_two = ext[1:2, :]
    h2 = (n2 * gain_two).astype(BF16)

    a, b, h2_all, gu, z, comb = call(
        moe_fwd_kernel,
        info,
        gather_group(h2, wm) + [wm, wext, chosen_all],
        [
            ((512, D), BF16),
            ((512, D), BF16),
            ((SEQ, D), BF16),
            ((SEQ, GU), F32),
            ((SEQ, DN), BF16),
            ((SEQ, EXT), F32),
        ],
        [((SEQ, D), BF16)],
        4_000_000_000,
        LIM[2],
    )
    y = x1 + scatter_group(a, b)
    diff = y - teach.astype(F32)
    squares = jnp.sum(diff * diff)
    dm = diff.astype(BF16)
    a, b, dm_all, dgu = call(
        moe_bwd_kernel,
        info,
        gather_group(dm) + [wm, gu, comb],
        [((512, D + EXT), BF16), ((512, D + EXT), BF16), ((SEQ, D), BF16), ((SEQ, GU), BF16)],
        [((SEQ, D + EXT), BF16)],
        4_000_000_000,
        LIM[3],
    )
    (dwm,) = call(
        moe_grad_kernel,
        info,
        [h2_all, dgu, dm_all, z],
        [((D, WM), BF16)],
        [((D, WM), BF16)],
        4_000_000_000,
        LIM[4],
        far_out=(0,),
        sems=2,
    )
    dwm_own = lax.psum_scatter(dwm, RING, scatter_dimension=0, tiled=True)
    dh2 = scatter_group(a, b)
    dcomb = dh2[:, D + 2 : D + 5] + dh2[:, D + 5 : D + 8]
    router = ext[2:5, :].astype(BF16)
    logits = lax.dot_general(h2, router, NT, preferred_element_type=F32)
    gates = jax.nn.softmax(logits, axis=1)
    dpick = dcomb * x_all[:, D + 2 : D + 5].astype(F32)
    dlogits = (gates * (dpick - jnp.sum(dpick * gates, axis=1, keepdims=True))).astype(BF16)
    d_router = lax.dot_general(dlogits, h2, TN, preferred_element_type=F32)
    dh2 = dh2[:, :D] + jnp.dot(dlogits, router, preferred_element_type=F32)
    d_ffn_gain = jnp.sum(dh2 * n2, axis=0, keepdims=True)
    g2 = dh2 * gain_two
    dx1 = diff + r2 * (g2 - n2 * jnp.mean(g2 * n2, axis=1, keepdims=True))
    da = dx1.astype(BF16)
    da_home = exchange(da)
    y_home = exchange(y.astype(BF16))

    sums = jnp.concatenate(
        [
            jnp.zeros((1, D), F32),
            d_ffn_gain,
            d_router,
            jnp.full((1, D), squares / (SEQ * 16), F32),
        ],
        axis=0,
    )
    sums = jnp.pad(sums, ((0, EXT - 6), (0, 0)))
    one = ((SEQ, HD), BF16)
    *a_blocks, dq0, dm1, gain = call(
        attn_bwd_kernel,
        info,
        gather_group(da)
        + [wo, k, q, v, mixed, h1, w, cos, sin, after(lse, da_home, y_home)],
        [((4 * PART, SPLIT_A), BF16)] * 4 + [((SEQ, SLOT), BF16), one, ((D, 1), F32)],
        [
            one,
            one,
            one,
            ((D, HW), BF16),
            head,
            ((SEQ, D), BF16),
            ((D, SLOT), BF16),
            ((SEQ, D), BF16),
            one,
            ((HD, SEQ), BF16),
            ((SEQ, HD), F32),
            ((SEQ, HD), F32),
            ((D, SPLIT_A), BF16),
        ],
        5_000_000_000,
        LIM[5],
        far_in=range(8, 15),
        sems=7,
    )
    *b_blocks, dq1 = call(
        attn_bwd_second_kernel,
        info,
        [dm1, k, q, v, mixed, h1, w, cos, sin, lse, gain, sums],
        [((4 * PART, WA - SPLIT_A), BF16)] * 4 + [((SEQ, SLOT), BF16)],
        [
            one,
            one,
            one,
            one,
            ((SEQ, D), BF16),
            ((D, SLOT + EXT), BF16),
            ((HD, SEQ), BF16),
            ((SEQ, HD), F32),
            ((SEQ, HD), F32),
            ((D, WA - SPLIT_A), BF16),
        ],
        3_000_000_000,
        LIM[7],
        far_in=range(1, 7),
        sems=7,
    )
    a, b = call(
        attn_in_kernel,
        info,
        [w, dq0, dq1],
        [((512, D), BF16), ((512, D), BF16)],
        [((SEQ, D), BF16)],
        2_000_000_000,
        LIM[6],
    )
    x = tokens.astype(F32)
    to_z = sum_cores(a, b)
    first = (
        add_parts([after(a_blocks[0], to_z)] + a_blocks[1:], along_y),
        add_parts([after(b_blocks[0], to_z)] + b_blocks[1:], along_x),
    )
    dwm_own = turn_home(after(dwm_own, first))
    cuts = [slice(i * PART, (i + 1) * PART) for i in range(4)]
    dw = jnp.concatenate(
        [
            add_parts([first[0][cut] for cut in cuts], along_x),
            add_parts([first[1][cut] for cut in cuts], along_y),
        ],
        axis=1,
    )
    dh1 = scatter_home(to_z)
    dw = lax.all_to_all(dw.reshape(8, n, WA), ("c", "z"), split_axis=0, concat_axis=0)
    dw = after(dw, dwm_own)
    d_qkv, d_out, d_gains, d_router, loss = call(
        finish_kernel,
        info,
        [dw],
        [((n, 3 * D), F32), ((n, D), F32), ((8, n), F32), ((n, 3), F32), ((1, 1), F32)],
        [],
        0,
        6,
    )

    r1 = lax.rsqrt(jnp.mean(x * x, axis=1, keepdims=True) + norm_eps)
    n1 = x * r1
    g1 = dh1 * ext[0:1, :]
    d_tokens = da_home.astype(F32) + r1 * (g1 - n1 * jnp.mean(g1 * n1, axis=1, keepdims=True))

    d_gu = dwm_own[:, :GU].reshape(-1, 4, 2, 128)[..., :UNITS].astype(F32)
    d_dn = dwm_own[:, GU:].reshape(-1, 4, 128)[..., :UNITS].astype(F32)
    return (
        y_home,
        loss.reshape(()),
        d_tokens,
        d_gains[0],
        d_qkv,
        d_out,
        d_router,
        d_gains[1],
        d_gu,
        d_dn,
    )


def solution(mesh):
    fine = Mesh(mesh.devices.reshape(4, 2, 2, 2, 4), ("y", "xl", "c", "xh", "z"))
    every = ("y", "xl", "c", "xh", "z")
    rows = P(every, None)
    in_specs = (
        rows,
        rows,
        P(),
        rows,
        P(every),
        rows,
        rows,
        rows,
        P(every),
        P(("y", "xl", "c"), None, None, ("xh", "z")),
        P(("y", "xl", "c"), None, ("xh", "z")),
    )
    out_specs = (
        rows,
        P(),
        rows,
        P(every),
        rows,
        rows,
        rows,
        P(every),
        P(("y", "xl", "c"), None, None, ("xh", "z")),
        P(("y", "xl", "c"), None, ("xh", "z")),
    )
    return jax.shard_map(
        on_device, mesh=fine, in_specs=in_specs, out_specs=out_specs, check_vma=False
    )
```

profile of v0, /device:TPU:1, one launch (start us, length us, event | category | flops | bytes accessed | tf_op | source)
XLA Modules:
  0.0 354.0 jit_solution(10302393775696017848)
XLA Ops:
  10.2 14.1 %all_to_all.10 = bf16[8,10,1152]{2,1,0:T(8,128)(2,1)S(1)} all-to-all(bf16[8,10,1152]{2,1,0:T(8,128)(2,1)S(1)} %fusion.9), channel_id=1, replica_groups=mesh['y'=4,'xl'=2,'c'=2,'xh'=2,'z'=4] {'c','z'}, dimensions={0} | all-to-all | bytes 368640 | tf_op jit(solution)/shard_map/all_to_all | solution.py:557
  25.3 4.9 %collective-permute-start = (bf16[128,1408]{1,0:T(8,128)(2,1)S(1)}, bf16[128,1408]{1,0:T(8,128)(2,1)S(1)}, u32[]{:S(2)}, u32[]{:S(2)}) collective-permute-start(bf16[128,1408]{1,0:T(8,128)(2,1)S(1)} %pad_maximum_fusion.2), channel_id=1, source_target_pairs={{0,0},{4,8},{8,4},{12,12},{1,1},{5,9},{9,5},{13,13},{2,2},{6,10},{... | collective-permute-start | bytes 1081352 | tf_op jit(solution)/shard_map/ppermute | solution.py:428
  30.3 5.6 %collective-permute-done.refs_0_ = bf16[128,1408]{1,0:T(8,128)(2,1)S(1)} collective-permute-done((bf16[128,1408]{1,0:T(8,128)(2,1)S(1)}, bf16[128,1408]{1,0:T(8,128)(2,1)S(1)}, u32[]{:S(2)}, u32[]{:S(2)}) %collective-permute-start) | collective-permute-done | bytes 360480 | tf_op jit(solution)/shard_map/ppermute | solution.py:428
  39.0 8.5 %collective-permute-done.1.refs_1_ = bf16[128,1408]{1,0:T(8,128)(2,1)S(1)} collective-permute-done((bf16[128,1408]{1,0:T(8,128)(2,1)S(1)}, bf16[128,1408]{1,0:T(8,128)(2,1)S(1)}, u32[]{:S(2)}, u32[]{:S(2)}) %collective-permute-start.1) | collective-permute-done | bytes 360480 | tf_op jit(solution)/shard_map/ppermute | solution.py:442
  59.4 12.1 %all-gather.3.cloned.1.call-done.w_far = bf16[1280,1152]{1,0:T(8,128)(2,1)} async-done(((bf16[80,1152]{1,0:T(8,128)(2,1)}), bf16[1280,1152]{1,0:T(8,128)(2,1)}) %all-gather.3.cloned.1.call-update) | async-done | bytes 2949136 | tf_op jit(solution)/shard_map/all_gather | solution.py:567
  75.0 17.5 %shard_map.187 = (bf16[1280,896]{1,0:T(8,128)(2,1)}, bf16[1024,1280]{1,0:T(8,128)(2,1)}, bf16[1024,256]{1,0:T(8,128)(2,1)S(1)}, bf16[1024,256]{1,0:T(8,128)(2,1)...) custom-call(s32[48]{0:T(128)S(1)} %stack.107.info, ...), custom_call_target="tpu_custom_call" | custom-call | flops 5000000000 | bytes 17924096 | tf_op jit(solution)/shard_map/pallas_call | solution.py:414
  102.7 11.7 %collective-permute-done.11 = bf16[128,1280]{1,0:T(8,128)(2,1)S(1)} collective-permute-done((bf16[128,1280]{1,0:T(8,128)(2,1)S(1)}, bf16[128,1280]{1,0:T(8,128)(2,1)S(1)}, u32[]{:S(2)}, u32[]{:S(2)}) %collective-permute-start.11) | collective-permute-done | bytes 327712 | tf_op jit(solution)/shard_map/ppermute | solution.py:442
  114.4 4.7 %collective-permute-done.9 = bf16[128,1280]{1,0:T(8,128)(2,1)S(1)} collective-permute-done((bf16[128,1280]{1,0:T(8,128)(2,1)S(1)}, bf16[128,1280]{1,0:T(8,128)(2,1)S(1)}, u32[]{:S(2)}, u32[]{:S(2)}) %collective-permute-start.9) | collective-permute-done | bytes 327712 | tf_op jit(solution)/shard_map/ppermute | solution.py:442
  125.4 13.1 %collective-permute-done.12.refs_1_ = bf16[128,1280]{1,0:T(8,128)(2,1)S(1)} collective-permute-done((bf16[128,1280]{1,0:T(8,128)(2,1)S(1)}, bf16[128,1280]{1,0:T(8,128)(2,1)S(1)}, u32[]{:S(2)}, u32[]{:S(2)}) %collective-permute-start.12) | collective-permute-done | bytes 327712 | tf_op jit(solution)/shard_map/ppermute | solution.py:442
  145.1 7.2 %shard_map.188 = (bf16[512,1280]{1,0:T(8,128)(2,1)S(1)}, bf16[512,1280]{1,0:T(8,128)(2,1)S(1)}, bf16[1024,1280]{1,0:T(8,128)(2,1)S(1)}, f32[1024,1024]{1,0:T(8,1...) custom-call(s32[48]{0:T(128)S(1)} %stack.107.info, bf16[128,1280]{1,0:T(8,128)(2,1)S(1)} %multiply_convert_fusion.refs_0_, ...), custom_call_target="tpu_custom_call" | custom-call | flops 4000000000 | bytes 18153472 | tf_op jit(solution)/shard_map/pallas_call | solution.py:414
  162.6 9.9 %collective-permute-done.23 = bf16[128,1280]{1,0:T(8,128)(2,1)S(1)} collective-permute-done((bf16[128,1280]{1,0:T(8,128)(2,1)S(1)}, bf16[128,1280]{1,0:T(8,128)(2,1)S(1)}, u32[]{:S(2)}, u32[]{:S(2)}) %collective-permute-start.23) | collective-permute-done | bytes 327712 | tf_op jit(solution)/shard_map/ppermute | solution.py:442
  181.0 6.9 %collective-permute-done.26.refs_1_ = bf16[128,1280]{1,0:T(8,128)(2,1)S(1)} collective-permute-done((bf16[128,1280]{1,0:T(8,128)(2,1)S(1)}, bf16[128,1280]{1,0:T(8,128)(2,1)S(1)}, u32[]{:S(2)}, u32[]{:S(2)}) %collective-permute-start.26) | collective-permute-done | bytes 327712 | tf_op jit(solution)/shard_map/ppermute | solution.py:442
  187.9 7.5 %collective-permute-start.30 = (bf16[128,1280]{1,0:T(8,128)(2,1)S(1)}, bf16[128,1280]{1,0:T(8,128)(2,1)S(1)}, u32[]{:S(2)}, u32[]{:S(2)}) collective-permute-start(bf16[128,1280]{1,0:T(8,128)(2,1)S(1)} %collective-permute-done.26.refs_1_), channel_id=1, source_target_pairs={{0,8},{8,0},{1,9},{9,1},{2,10},{10,2},{3,11},{11,3},{4,12},{12,4},... | collective-permute-start | bytes 983048 | tf_op jit(solution)/shard_map/ppermute | solution.py:466
  197.6 7.0 %shard_map.189 = (bf16[512,1408]{1,0:T(8,128)(2,1)S(1)}, bf16[512,1408]{1,0:T(8,128)(2,1)S(1)}, bf16[1024,1280]{1,0:T(8,128)(2,1)S(1)}, bf16[1024,1024]{1,0:T(8,128)(2,1)S(1)}) custom-call(s32[48]{0:T(128)S(1)} %stack.107.info, bf16[128,1280]{1,0:T(8,128)(2,1)S(1)} %fusion.11.refs_0_, bf16[128,1280]{1,0:T(8,128)(2,1)S(1)} %collective-permute-done.26.refs_1_, ...), custom_call_target="tpu_custom_call" | custom-call | flops 4000000000 | bytes 18874368 | tf_op jit(solution)/shard_map/pallas_call | solution.py:414
  212.1 5.6 %shard_map.193 = bf16[1280,1536]{1,0:T(8,128)(2,1)S(1)} custom-call(s32[48]{0:T(128)S(1)} %stack.107.info, bf16[1024,1280]{1,0:T(8,128)(2,1)S(1)} %get-tuple-element.99.refs_0_, bf16[1024,1024]{1,0:T(8,128)(2,1)S(1)} %get-tuple-element.100.refs_1_, bf16[1024,1280]{1,0:T(8,128)(2,1)S(1)} %get-tuple-element.101.refs_2_, ...), custom_call_target="tpu_custom_call" | custom-call | flops 4000000000 | bytes 12320768 | tf_op jit(solution)/shard_map/pallas_call | solution.py:414
  222.2 8.7 %collective-permute-done.34 = bf16[128,1408]{1,0:T(8,128)(2,1)} collective-permute-done((bf16[128,1408]{1,0:T(8,128)(2,1)}, bf16[128,1408]{1,0:T(8,128)(2,1)}, u32[]{:S(2)}, u32[]{:S(2)}) %collective-permute-start.34) | collective-permute-done | bytes 360480 | tf_op jit(solution)/shard_map/ppermute | solution.py:442
  241.7 5.2 %collective-permute-done.24 = bf16[128,1280]{1,0:T(8,128)(2,1)S(1)} collective-permute-done((bf16[128,1280]{1,0:T(8,128)(2,1)}, bf16[128,1280]{1,0:T(8,128)(2,1)S(1)}, u32[]{:S(2)}, u32[]{:S(2)}) %collective-permute-start.24) | collective-permute-done | bytes 327712 | tf_op jit(solution)/shard_map/ppermute | solution.py:428
  250.5 5.2 %collective-permute-done.37.refs_1_ = bf16[128,1280]{1,0:T(8,128)(2,1)S(1)} collective-permute-done((bf16[128,1280]{1,0:T(8,128)(2,1)S(1)}, bf16[128,1280]{1,0:T(8,128)(2,1)S(1)}, u32[]{:S(2)}, u32[]{:S(2)}) %collective-permute-start.37) | collective-permute-done | bytes 327712 | tf_op jit(solution)/shard_map/ppermute | solution.py:442
  258.8 10.7 %shard_map.190 = (bf16[320,640]{1,0:T(8,128)(2,1)S(1)}, bf16[320,640]{1,0:T(8,128)(2,1)S(1)}, bf16[320,640]{1,0:T(8,128)(2,1)}, bf16[320,640]{1,0:T(8,128)(2,1)}...) custom-call(s32[48]{0:T(128)S(1)} %stack.107.info, ...), custom_call_target="tpu_custom_call" | custom-call | flops 5000000000 | bytes 14062592 | tf_op jit(solution)/shard_map/pallas_call | solution.py:414
  269.5 7.0 %shard_map.191 = (bf16[320,512]{1,0:T(8,128)(2,1)S(1)}, bf16[320,512]{1,0:T(8,128)(2,1)S(1)}, bf16[320,512]{1,0:T(8,128)(2,1)S(1)}, bf16[320,512]{1,0:T(8,128)(2,1)S(1)}, bf16[1024,384]{1,0:T(8,128)(2,1)}) custom-call(s32[48]{0:T(128)S(1)} %stack.107.info, bf16[1024,128]{1,0:T(8,128)(2,1)S(1)} %get-tuple-element.85.refs_0_, bf16[1024,256]{1,0:T(8,128)(2,1)S(1)} %copy-done.9, ...), custom_call_target="tpu_custom_call" | custom-call | flops 3000000000 | bytes 11113472 | tf_op jit(solution)/shard_map/pallas_call | solution.py:414
  287.9 4.0 %collective-permute-done.54 = bf16[320,512]{1,0:T(8,128)(2,1)S(1)} collective-permute-done((bf16[320,512]{1,0:T(8,128)(2,1)S(1)}, bf16[320,512]{1,0:T(8,128)(2,1)S(1)}, u32[]{:S(2)}, u32[]{:S(2)}) %collective-permute-start.54) | collective-permute-done | bytes 327712 | tf_op jit(solution)/shard_map/ppermute | solution.py:451
  295.5 8.7 %collective-permute-start.62 = (bf16[128,1280]{1,0:T(8,128)(2,1)}, bf16[128,1280]{1,0:T(8,128)(2,1)S(1)}, u32[]{:S(2)}, u32[]{:S(2)}) collective-permute-start(bf16[128,1280]{1,0:T(8,128)(2,1)} %get-tuple-element.161), channel_id=1, source_target_pairs={{0,3},{1,0},{2,1},{3,2},{4,11},{5,8},{6,9},{7,10},{8,7},{9,4},{10,... | collective-permute-start | bytes 983048 | tf_op jit(solution)/shard_map/ppermute | solution.py:502
  317.0 4.9 %collective-permute-start.60 = (bf16[128,1280]{1,0:T(8,128)(2,1)}, bf16[128,1280]{1,0:T(8,128)(2,1)S(1)}, u32[]{:S(2)}, u32[]{:S(2)}) collective-permute-start(bf16[128,1280]{1,0:T(8,128)(2,1)} %get-tuple-element.163), channel_id=1, source_target_pairs={{0,1},{1,2},{2,3},{3,0},{4,9},{5,10},{6,11},{7,8},{8,5},{9,6},{10,... | collective-permute-start | bytes 983048 | tf_op jit(solution)/shard_map/ppermute | solution.py:502
  326.5 7.7 %all-to-all-start.1 = ((bf16[8,10,1152]{2,1,0:T(8,128)(2,1)}), bf16[8,10,1152]{2,1,0:T(8,128)(2,1)S(1)}, u32[]{:S(2)}, u32[]{:S(2)}) async-start(bf16[8,10,1152]{2,1,0:T(8,128)(2,1)} %reshape.94), calls=%async_computation.1 | async-start | bytes 589824 | tf_op jit(solution)/shard_map/all_to_all | solution.py:766
  (264 shorter events, 139.7 us)
Async XLA Ops:
  7.2 64.3 %all-gather.3.cloned.1.call-start = ((), (), s32[]{:S(2)}) async-start(), calls=%async_computation.3 | async-start | bytes 3133440 | tf_op jit(solution)/shard_map/all_gather | solution.py:567
  25.1 114.7 %all-gather.5.cloned.1.call-start = ((), (), s32[]{:S(2)}) async-start(), calls=%async_computation.4 | async-start | bytes 4177920 | tf_op jit(solution)/shard_map/all_gather | solution.py:577
  71.5 263.1 %reduce-scatter.2.cloned.1.call-start = ((), (), s32[]{:S(2)}) async-start(), calls=%async_computation.5 | async-start | bytes 4177920 | tf_op jit(solution)/shard_map/reduce_scatter | solution.py:665
  101.2 17.8 %collective-permute-start.9 = (bf16[128,1280]{1,0:T(8,128)(2,1)S(1)}, bf16[128,1280]{1,0:T(8,128)(2,1)S(1)}, u32[]{:S(2)}, u32[]{:S(2)}) collective-permute-start(bf16[128,1280]{1,0:T(8,128)(2,1)S(1)} %get-tuple-element.168), channel_id=1, source_target_pairs={{0,1},{1,2},{2,3},{3,0},{4,5},{5,6},{6,7},{7,4},{8,9},{9,10},{10,1... | collective-permute-start | bytes 983048 | tf_op jit(solution)/shard_map/ppermute | solution.py:442
  121.3 17.2 %collective-permute-start.12 = (bf16[128,1280]{1,0:T(8,128)(2,1)S(1)}, bf16[128,1280]{1,0:T(8,128)(2,1)S(1)}, u32[]{:S(2)}, u32[]{:S(2)}) collective-permute-start(bf16[128,1280]{1,0:T(8,128)(2,1)S(1)} %multiply_convert_fusion.refs_0_), channel_id=1, source_target_pairs={{0,1},{1,2},{2,3},{3,0},{4,5},{5,6},{6,7},{7,4},{8,9},{9,10},{10,1... | collective-permute-start | bytes 983048 | tf_op jit(solution)/shard_map/ppermute | solution.py:442
  121.4 18.3 %collective-permute-start.13 = (bf16[128,1280]{1,0:T(8,128)(2,1)S(1)}, bf16[128,1280]{1,0:T(8,128)(2,1)S(1)}, u32[]{:S(2)}, u32[]{:S(2)}) collective-permute-start(bf16[128,1280]{1,0:T(8,128)(2,1)S(1)} %multiply_convert_fusion.refs_0_), channel_id=1, source_target_pairs={{0,2},{1,3},{2,0},{3,1},{4,6},{5,7},{6,4},{7,5},{8,10},{9,11},{10,... | collective-permute-start | bytes 983048 | tf_op jit(solution)/shard_map/ppermute | solution.py:442
  121.9 17.8 %collective-permute-start.14 = (bf16[128,1280]{1,0:T(8,128)(2,1)S(1)}, bf16[128,1280]{1,0:T(8,128)(2,1)S(1)}, u32[]{:S(2)}, u32[]{:S(2)}) collective-permute-start(bf16[128,1280]{1,0:T(8,128)(2,1)S(1)} %multiply_convert_fusion.refs_0_), channel_id=1, source_target_pairs={{0,3},{1,0},{2,1},{3,2},{4,7},{5,4},{6,5},{7,6},{8,11},{9,8},{10,9... | collective-permute-start | bytes 983048 | tf_op jit(solution)/shard_map/ppermute | solution.py:442
  156.2 16.3 %collective-permute-start.23 = (bf16[128,1280]{1,0:T(8,128)(2,1)S(1)}, bf16[128,1280]{1,0:T(8,128)(2,1)S(1)}, u32[]{:S(2)}, u32[]{:S(2)}) collective-permute-start(bf16[128,1280]{1,0:T(8,128)(2,1)S(1)} %get-tuple-element.166), channel_id=1, source_target_pairs={{0,3},{1,0},{2,1},{3,2},{4,7},{5,4},{6,5},{7,6},{8,11},{9,8},{10,9... | collective-permute-start | bytes 983048 | tf_op jit(solution)/shard_map/ppermute | solution.py:442
  158.3 17.6 %collective-permute-start.21 = (bf16[128,1280]{1,0:T(8,128)(2,1)S(1)}, bf16[128,1280]{1,0:T(8,128)(2,1)S(1)}, u32[]{:S(2)}, u32[]{:S(2)}) collective-permute-start(bf16[128,1280]{1,0:T(8,128)(2,1)S(1)} %get-tuple-element.165), channel_id=1, source_target_pairs={{0,1},{1,2},{2,3},{3,0},{4,5},{5,6},{6,7},{7,4},{8,9},{9,10},{10,1... | collective-permute-start | bytes 983048 | tf_op jit(solution)/shard_map/ppermute | solution.py:442
  177.1 18.3 %collective-permute-start.27 = (bf16[128,1280]{1,0:T(8,128)(2,1)S(1)}, bf16[128,1280]{1,0:T(8,128)(2,1)S(1)}, u32[]{:S(2)}, u32[]{:S(2)}) collective-permute-start(bf16[128,1280]{1,0:T(8,128)(2,1)S(1)} %fusion.11.refs_0_), channel_id=1, source_target_pairs={{0,2},{1,3},{2,0},{3,1},{4,6},{5,7},{6,4},{7,5},{8,10},{9,11},{10,... | collective-permute-start | bytes 983048 | tf_op jit(solution)/shard_map/ppermute | solution.py:442
  178.7 16.7 %collective-permute-start.28 = (bf16[128,1280]{1,0:T(8,128)(2,1)S(1)}, bf16[128,1280]{1,0:T(8,128)(2,1)S(1)}, u32[]{:S(2)}, u32[]{:S(2)}) collective-permute-start(bf16[128,1280]{1,0:T(8,128)(2,1)S(1)} %fusion.11.refs_0_), channel_id=1, source_target_pairs={{0,3},{1,0},{2,1},{3,2},{4,7},{5,4},{6,5},{7,6},{8,11},{9,8},{10,9... | collective-permute-start | bytes 983048 | tf_op jit(solution)/shard_map/ppermute | solution.py:442
  179.7 16.3 %collective-permute-start.29 = (bf16[128,1280]{1,0:T(8,128)(2,1)S(1)}, bf16[128,1280]{1,0:T(8,128)(2,1)S(1)}, u32[]{:S(2)}, u32[]{:S(2)}) collective-permute-start(bf16[128,1280]{1,0:T(8,128)(2,1)S(1)} %fusion.11.refs_0_), channel_id=1, source_target_pairs={{0,8},{8,0},{1,9},{9,1},{2,10},{10,2},{3,11},{11,3},{4,12},{12,4},... | collective-permute-start | bytes 983048 | tf_op jit(solution)/shard_map/ppermute | solution.py:466
  211.0 19.9 %collective-permute-start.34 = (bf16[128,1408]{1,0:T(8,128)(2,1)}, bf16[128,1408]{1,0:T(8,128)(2,1)}, u32[]{:S(2)}, u32[]{:S(2)}) collective-permute-start(bf16[128,1408]{1,0:T(8,128)(2,1)} %get-tuple-element.158), channel_id=1, source_target_pairs={{0,1},{1,2},{2,3},{3,0},{4,5},{5,6},{6,7},{7,4},{8,9},{9,10},{10,1... | collective-permute-start | bytes 1081352 | tf_op jit(solution)/shard_map/ppermute | solution.py:442
  237.9 17.7 %collective-permute-start.37 = (bf16[128,1280]{1,0:T(8,128)(2,1)S(1)}, bf16[128,1280]{1,0:T(8,128)(2,1)S(1)}, u32[]{:S(2)}, u32[]{:S(2)}) collective-permute-start(bf16[128,1280]{1,0:T(8,128)(2,1)S(1)} %get-tuple-element.171.refs_0_), channel_id=1, source_target_pairs={{0,1},{1,2},{2,3},{3,0},{4,5},{5,6},{6,7},{7,4},{8,9},{9,10},{10,1... | collective-permute-start | bytes 983048 | tf_op jit(solution)/shard_map/ppermute | solution.py:442
  238.0 17.7 %collective-permute-start.38 = (bf16[128,1280]{1,0:T(8,128)(2,1)S(1)}, bf16[128,1280]{1,0:T(8,128)(2,1)S(1)}, u32[]{:S(2)}, u32[]{:S(2)}) collective-permute-start(bf16[128,1280]{1,0:T(8,128)(2,1)S(1)} %get-tuple-element.171.refs_0_), channel_id=1, source_target_pairs={{0,2},{1,3},{2,0},{3,1},{4,6},{5,7},{6,4},{7,5},{8,10},{9,11},{10,... | collective-permute-start | bytes 983048 | tf_op jit(solution)/shard_map/ppermute | solution.py:442
  239.5 17.1 %collective-permute-start.39 = (bf16[128,1280]{1,0:T(8,128)(2,1)S(1)}, bf16[128,1280]{1,0:T(8,128)(2,1)S(1)}, u32[]{:S(2)}, u32[]{:S(2)}) collective-permute-start(bf16[128,1280]{1,0:T(8,128)(2,1)S(1)} %get-tuple-element.171.refs_0_), channel_id=1, source_target_pairs={{0,3},{1,0},{2,1},{3,2},{4,7},{5,4},{6,5},{7,6},{8,11},{9,8},{10,9... | collective-permute-start | bytes 983048 | tf_op jit(solution)/shard_map/ppermute | solution.py:442
  241.4 17.3 %collective-permute-start.40 = (bf16[128,1280]{1,0:T(8,128)(2,1)S(1)}, bf16[128,1280]{1,0:T(8,128)(2,1)S(1)}, u32[]{:S(2)}, u32[]{:S(2)}) collective-permute-start(bf16[128,1280]{1,0:T(8,128)(2,1)S(1)} %get-tuple-element.171.refs_0_), channel_id=1, source_target_pairs={{0,8},{8,0},{1,9},{9,1},{2,10},{10,2},{3,11},{11,3},{4,12},{12,4},... | collective-permute-start | bytes 983048 | tf_op jit(solution)/shard_map/ppermute | solution.py:466
  285.1 20.0 %collective-permute-start.52 = (bf16[320,512]{1,0:T(8,128)(2,1)S(1)}, bf16[320,512]{1,0:T(8,128)(2,1)S(1)}, u32[]{:S(2)}, u32[]{:S(2)}) collective-permute-start(bf16[320,512]{1,0:T(8,128)(2,1)S(1)} %get-tuple-element.96), channel_id=1, source_target_pairs={{0,16},{16,4},{4,20},{20,0},{1,17},{17,5},{5,21},{21,1},{2,18},{18... | collective-permute-start | bytes 983048 | tf_op jit(solution)/shard_map/ppermute | solution.py:451
  285.1 21.2 %collective-permute-start.48 = (bf16[320,640]{1,0:T(8,128)(2,1)S(1)}, bf16[320,640]{1,0:T(8,128)(2,1)S(1)}, u32[]{:S(2)}, u32[]{:S(2)}) collective-permute-start(bf16[320,640]{1,0:T(8,128)(2,1)S(1)} %copy-done.30), channel_id=1, source_target_pairs={{0,96},{32,0},{64,32},{96,64},{1,97},{33,1},{65,33},{97,65},{2,98}... | collective-permute-start | bytes 1228808 | tf_op jit(solution)/shard_map/ppermute | solution.py:446
  286.0 21.7 %collective-permute-start.47 = (bf16[320,640]{1,0:T(8,128)(2,1)S(1)}, bf16[320,640]{1,0:T(8,128)(2,1)S(1)}, u32[]{:S(2)}, u32[]{:S(2)}) collective-permute-start(bf16[320,640]{1,0:T(8,128)(2,1)S(1)} %copy-done.29), channel_id=1, source_target_pairs={{0,64},{32,96},{64,0},{96,32},{1,65},{33,97},{65,1},{97,33},{2,66}... | collective-permute-start | bytes 1228808 | tf_op jit(solution)/shard_map/ppermute | solution.py:446
  292.0 18.1 %collective-permute-start.46 = (bf16[320,640]{1,0:T(8,128)(2,1)S(1)}, bf16[320,640]{1,0:T(8,128)(2,1)S(1)}, u32[]{:S(2)}, u32[]{:S(2)}) collective-permute-start(bf16[320,640]{1,0:T(8,128)(2,1)S(1)} %get-tuple-element.91), channel_id=1, source_target_pairs={{0,32},{32,64},{64,96},{96,0},{1,33},{33,65},{65,97},{97,1},{2,34}... | collective-permute-start | bytes 1228808 | tf_op jit(solution)/shard_map/ppermute | solution.py:446
  295.5 38.7 %collective-permute-start.62 = (bf16[128,1280]{1,0:T(8,128)(2,1)}, bf16[128,1280]{1,0:T(8,128)(2,1)S(1)}, u32[]{:S(2)}, u32[]{:S(2)}) collective-permute-start(bf16[128,1280]{1,0:T(8,128)(2,1)} %get-tuple-element.161), channel_id=1, source_target_pairs={{0,3},{1,0},{2,1},{3,2},{4,11},{5,8},{6,9},{7,10},{8,7},{9,4},{10,... | collective-permute-start | bytes 983048 | tf_op jit(solution)/shard_map/ppermute | solution.py:502
  305.1 29.2 %collective-permute-start.61 = (bf16[128,1280]{1,0:T(8,128)(2,1)}, bf16[128,1280]{1,0:T(8,128)(2,1)S(1)}, u32[]{:S(2)}, u32[]{:S(2)}) collective-permute-start(bf16[128,1280]{1,0:T(8,128)(2,1)} %get-tuple-element.162), channel_id=1, source_target_pairs={{0,2},{1,3},{2,0},{3,1},{4,10},{5,11},{6,8},{7,9},{8,6},{9,7},{10,... | collective-permute-start | bytes 983048 | tf_op jit(solution)/shard_map/ppermute | solution.py:502
  317.0 17.2 %collective-permute-start.60 = (bf16[128,1280]{1,0:T(8,128)(2,1)}, bf16[128,1280]{1,0:T(8,128)(2,1)S(1)}, u32[]{:S(2)}, u32[]{:S(2)}) collective-permute-start(bf16[128,1280]{1,0:T(8,128)(2,1)} %get-tuple-element.163), channel_id=1, source_target_pairs={{0,1},{1,2},{2,3},{3,0},{4,9},{5,10},{6,11},{7,8},{8,5},{9,6},{10,... | collective-permute-start | bytes 983048 | tf_op jit(solution)/shard_map/ppermute | solution.py:502
  (76 other events, 699.7 us)
Sparse Core Ops, SparseCore 0:
  25.2 46.2 all-gather.2
  74.2 50.3 all-gather.4
  219.8 86.3 reduce-scatter.1
where the time goes:
time: 359 us; the launch traced here: 354 us
  waiting for transfers between devices  126 us (35%)
  starting transfers between devices  98.5 us (27%)
  Pallas kernels  60.7 us (17%)
  other arithmetic  18.5 us (5%)
  local copies, waits for them, and re-layouts  18.1 us (5%)
  between operations  15.8 us (4%)
  blocking collectives  14.1 us (4%)
    ppermute x21, waiting for transfers between devices, along_z(): return lax.ppermute(x, 'z', [(i, (i + k) % 4) for i in range(4)])  73.7 us
    pallas_call x9, Pallas kernels, call(): pl.pallas_call(kernel, out_shape=[jax.ShapeDtypeStruct(s, t) for s, t in...  60.7 us
    ppermute x21, starting transfers between devices, along_z(): return lax.ppermute(x, 'z', [(i, (i + k) % 4) for i in range(4)])  20.3 us
    ppermute x4, starting transfers between devices, scatter_home(): total = total + lax.ppermute(parts[k], ('c', 'xh', 'z'), pairs).astype(F32)  18.3 us
    ppermute x20, starting transfers between devices, to_other_core(): return lax.ppermute(x, 'c', [(0, 1), (1, 0)])  16.1 us
    ppermute x4, waiting for transfers between devices, exchange(): return lax.ppermute(x, ('c', 'xh'), [(0, 0), (1, 2), (2, 1), (3, 3)])  15.2 us
    ppermute x4, starting transfers between devices, exchange(): return lax.ppermute(x, ('c', 'xh'), [(0, 0), (1, 2), (2, 1), (3, 3)])  14.7 us
    all_to_all x1, blocking collectives, on_device(): lax.all_to_all(packed, ('c', 'z'), split_axis=0, concat_axis=0)  14.1 us
  transfers between devices with their start and end apart: 67, of which 31 were waited for; matrix products, arithmetic and copies ran while one was open for 6% of the time, Pallas kernels for 13%

commit v1 on v0

--- a/solution.py
+++ b/solution.py
@@ -174,7 +174,7 @@
     for i in range(8):
         h2[rows_of(info[i] * ROWS), :] = hs[i][...]
 
-    @pl.loop(0, 4)
+    @pl.loop(0, 4, unroll=True)
     def _(step):
         at = rows_of(step * 256, 256)
         h = h2[at, :]
@@ -208,7 +208,7 @@
     for i in range(8):
         dm[rows_of(info[i] * ROWS), :] = ds[i][...]
 
-    @pl.loop(0, 4)
+    @pl.loop(0, 4, unroll=True)
     def _(step):
         at = rows_of(step * 256, 256)
         dz = dot(dm[at, :], wm[:, GU:])
@@ -574,9 +574,9 @@
         0,
         6,
     )
-    wm = lax.all_gather(after(wm_own, w_all, x_seq), RING, axis=0, tiled=True)
+    cos, sin = rope_tables()
+    wm = lax.all_gather(after(wm_own, w_all, x_seq, cos, sin), RING, axis=0, tiled=True)
     teach = exchange(teacher)
-    cos, sin = rope_tables()
 
     head = ((SEQ, HW), BF16)
     w, h1, q, k, v, mixed, wo, a, b, wext, lse, ext = call(

time: 359 us -> 355 us (0.989)
  starting transfers between devices: 98.5 us -> 87.1 us
  waiting for transfers between devices: 126 us -> 131 us
    ppermute x6, waiting for transfers between devices: 7.69 us -> 13.5 us  [along_x(): lax.ppermute(x, ('xl', 'xh'), [(place[i], place[(i + k) % 4]) for i in ra...]
    ppermute x6, starting transfers between devices: 8.48 us -> 4.13 us  [along_x(): lax.ppermute(x, ('xl', 'xh'), [(place[i], place[(i + k) % 4]) for i in ra...]
    ppermute x6, waiting for transfers between devices: 0.42 us -> 4.59 us  [along_y(): return lax.ppermute(x, 'y', [(i, (i + k) % 4) for i in range(4)])]
  transfers between devices with their start and end apart: 67 -> 67, of which waited for: 31 -> 35; matrix products, arithmetic and copies ran while one was open for 6% -> 7% of each run, Pallas kernels for 13% -> 13%
where the time goes in v1:
time: 355 us; the launch traced here: 348 us
  waiting for transfers between devices  131 us (37%)
  starting transfers between devices  87.1 us (25%)
  Pallas kernels  58.8 us (17%)
  other arithmetic  21.2 us (6%)
  local copies, waits for them, and re-layouts  18.3 us (5%)
  between operations  15.7 us (4%)
  blocking collectives  14.1 us (4%)
    ppermute x21, waiting for transfers between devices, along_z(): return lax.ppermute(x, 'z', [(i, (i + k) % 4) for i in range(4)])  72.4 us
    pallas_call x9, Pallas kernels, call(): pl.pallas_call(kernel, out_shape=[jax.ShapeDtypeStruct(s, t) for s, t in...  58.8 us
    ppermute x21, starting transfers between devices, along_z(): return lax.ppermute(x, 'z', [(i, (i + k) % 4) for i in range(4)])  20 us
    ppermute x20, starting transfers between devices, to_other_core(): return lax.ppermute(x, 'c', [(0, 1), (1, 0)])  16.5 us
    ppermute x4, starting transfers between devices, scatter_home(): total = total + lax.ppermute(parts[k], ('c', 'xh', 'z'), pairs).astype(F32)  15.9 us
    ppermute x4, starting transfers between devices, exchange(): return lax.ppermute(x, ('c', 'xh'), [(0, 0), (1, 2), (2, 1), (3, 3)])  14.8 us
    all_gather x1, waiting for transfers between devices, on_device(): w_all = lax.all_gather(packed, RING, axis=0, tiled=True)  14.7 us
    all_to_all x1, blocking collectives, on_device(): lax.all_to_all(packed, ('c', 'z'), split_axis=0, concat_axis=0)  14.1 us
  transfers between devices with their start and end apart: 67, of which 35 were waited for; matrix products, arithmetic and copies ran while one was open for 7% of the time, Pallas kernels for 13%

profile of v1, /device:TPU:1, one launch (start us, length us, event | category | flops | bytes accessed | tf_op | source)
XLA Modules:
  0.0 348.1 jit_solution(11865307132753468788)
XLA Ops:
  10.2 14.1 %all_to_all.10 = bf16[8,10,1152]{2,1,0:T(8,128)(2,1)S(1)} all-to-all(bf16[8,10,1152]{2,1,0:T(8,128)(2,1)S(1)} %fusion.9), channel_id=1, replica_groups=mesh['y'=4,'xl'=2,'c'=2,'xh'=2,'z'=4] {'c','z'}, dimensions={0} | all-to-all | bytes 368640 | tf_op jit(solution)/shard_map/all_to_all | solution.py:557
  25.3 4.9 %collective-permute-start = (bf16[128,1408]{1,0:T(8,128)(2,1)S(1)}, bf16[128,1408]{1,0:T(8,128)(2,1)S(1)}, u32[]{:S(2)}, u32[]{:S(2)}) collective-permute-start(bf16[128,1408]{1,0:T(8,128)(2,1)S(1)} %pad_maximum_fusion.2), channel_id=1, source_target_pairs={{0,0},{4,8},{8,4},{12,12},{1,1},{5,9},{9,5},{13,13},{2,2},{6,10},{... | collective-permute-start | bytes 1081352 | tf_op jit(solution)/shard_map/ppermute | solution.py:428
  30.6 5.2 %collective-permute-done.refs_0_ = bf16[128,1408]{1,0:T(8,128)(2,1)S(1)} collective-permute-done((bf16[128,1408]{1,0:T(8,128)(2,1)S(1)}, bf16[128,1408]{1,0:T(8,128)(2,1)S(1)}, u32[]{:S(2)}, u32[]{:S(2)}) %collective-permute-start) | collective-permute-done | bytes 360480 | tf_op jit(solution)/shard_map/ppermute | solution.py:428
  41.3 6.3 %collective-permute-done.1.refs_1_ = bf16[128,1408]{1,0:T(8,128)(2,1)S(1)} collective-permute-done((bf16[128,1408]{1,0:T(8,128)(2,1)S(1)}, bf16[128,1408]{1,0:T(8,128)(2,1)S(1)}, u32[]{:S(2)}, u32[]{:S(2)}) %collective-permute-start.1) | collective-permute-done | bytes 360480 | tf_op jit(solution)/shard_map/ppermute | solution.py:442
  58.0 14.7 %all-gather.3.cloned.1.call-done.w_far = bf16[1280,1152]{1,0:T(8,128)(2,1)} async-done(((bf16[80,1152]{1,0:T(8,128)(2,1)}), bf16[1280,1152]{1,0:T(8,128)(2,1)}) %all-gather.3.cloned.1.call-update) | async-done | bytes 2949136 | tf_op jit(solution)/shard_map/all_gather | solution.py:567
  73.0 17.6 %shard_map.187 = (bf16[1280,896]{1,0:T(8,128)(2,1)}, bf16[1024,1280]{1,0:T(8,128)(2,1)}, bf16[1024,256]{1,0:T(8,128)(2,1)S(1)}, bf16[1024,256]{1,0:T(8,128)(2,1)...) custom-call(s32[48]{0:T(128)S(1)} %stack.107.info, ...), custom_call_target="tpu_custom_call" | custom-call | flops 5000000000 | bytes 17924096 | tf_op jit(solution)/shard_map/pallas_call | solution.py:414
  100.8 11.7 %collective-permute-done.11 = bf16[128,1280]{1,0:T(8,128)(2,1)S(1)} collective-permute-done((bf16[128,1280]{1,0:T(8,128)(2,1)S(1)}, bf16[128,1280]{1,0:T(8,128)(2,1)S(1)}, u32[]{:S(2)}, u32[]{:S(2)}) %collective-permute-start.11) | collective-permute-done | bytes 327712 | tf_op jit(solution)/shard_map/ppermute | solution.py:442
  112.5 4.7 %collective-permute-done.9 = bf16[128,1280]{1,0:T(8,128)(2,1)S(1)} collective-permute-done((bf16[128,1280]{1,0:T(8,128)(2,1)S(1)}, bf16[128,1280]{1,0:T(8,128)(2,1)S(1)}, u32[]{:S(2)}, u32[]{:S(2)}) %collective-permute-start.9) | collective-permute-done | bytes 327712 | tf_op jit(solution)/shard_map/ppermute | solution.py:442
  123.2 13.4 %collective-permute-done.12.refs_1_ = bf16[128,1280]{1,0:T(8,128)(2,1)S(1)} collective-permute-done((bf16[128,1280]{1,0:T(8,128)(2,1)S(1)}, bf16[128,1280]{1,0:T(8,128)(2,1)S(1)}, u32[]{:S(2)}, u32[]{:S(2)}) %collective-permute-start.12) | collective-permute-done | bytes 327712 | tf_op jit(solution)/shard_map/ppermute | solution.py:442
  143.2 6.1 %shard_map.188 = (bf16[512,1280]{1,0:T(8,128)(2,1)S(1)}, bf16[512,1280]{1,0:T(8,128)(2,1)S(1)}, bf16[1024,1280]{1,0:T(8,128)(2,1)S(1)}, f32[1024,1024]{1,0:T(8,1...) custom-call(s32[48]{0:T(128)S(1)} %stack.107.info, bf16[128,1280]{1,0:T(8,128)(2,1)S(1)} %multiply_convert_fusion.refs_0_, ...), custom_call_target="tpu_custom_call" | custom-call | flops 4000000000 | bytes 18153472 | tf_op jit(solution)/shard_map/pallas_call | solution.py:414
  159.7 10.0 %collective-permute-done.23 = bf16[128,1280]{1,0:T(8,128)(2,1)S(1)} collective-permute-done((bf16[128,1280]{1,0:T(8,128)(2,1)S(1)}, bf16[128,1280]{1,0:T(8,128)(2,1)S(1)}, u32[]{:S(2)}, u32[]{:S(2)}) %collective-permute-start.23) | collective-permute-done | bytes 327712 | tf_op jit(solution)/shard_map/ppermute | solution.py:442
  178.1 6.9 %collective-permute-done.26.refs_1_ = bf16[128,1280]{1,0:T(8,128)(2,1)S(1)} collective-permute-done((bf16[128,1280]{1,0:T(8,128)(2,1)S(1)}, bf16[128,1280]{1,0:T(8,128)(2,1)S(1)}, u32[]{:S(2)}, u32[]{:S(2)}) %collective-permute-start.26) | collective-permute-done | bytes 327712 | tf_op jit(solution)/shard_map/ppermute | solution.py:442
  185.0 7.5 %collective-permute-start.30 = (bf16[128,1280]{1,0:T(8,128)(2,1)S(1)}, bf16[128,1280]{1,0:T(8,128)(2,1)S(1)}, u32[]{:S(2)}, u32[]{:S(2)}) collective-permute-start(bf16[128,1280]{1,0:T(8,128)(2,1)S(1)} %collective-permute-done.26.refs_1_), channel_id=1, source_target_pairs={{0,8},{8,0},{1,9},{9,1},{2,10},{10,2},{3,11},{11,3},{4,12},{12,4},... | collective-permute-start | bytes 983048 | tf_op jit(solution)/shard_map/ppermute | solution.py:466
  194.7 6.1 %shard_map.189 = (bf16[512,1408]{1,0:T(8,128)(2,1)S(1)}, bf16[512,1408]{1,0:T(8,128)(2,1)S(1)}, bf16[1024,1280]{1,0:T(8,128)(2,1)S(1)}, bf16[1024,1024]{1,0:T(8,128)(2,1)S(1)}) custom-call(s32[48]{0:T(128)S(1)} %stack.107.info, bf16[128,1280]{1,0:T(8,128)(2,1)S(1)} %fusion.11.refs_0_, bf16[128,1280]{1,0:T(8,128)(2,1)S(1)} %collective-permute-done.26.refs_1_, ...), custom_call_target="tpu_custom_call" | custom-call | flops 4000000000 | bytes 18874368 | tf_op jit(solution)/shard_map/pallas_call | solution.py:414
  208.1 5.6 %shard_map.193 = bf16[1280,1536]{1,0:T(8,128)(2,1)S(1)} custom-call(s32[48]{0:T(128)S(1)} %stack.107.info, bf16[1024,1280]{1,0:T(8,128)(2,1)S(1)} %get-tuple-element.99.refs_0_, bf16[1024,1024]{1,0:T(8,128)(2,1)S(1)} %get-tuple-element.100.refs_1_, bf16[1024,1280]{1,0:T(8,128)(2,1)S(1)} %get-tuple-element.101.refs_2_, ...), custom_call_target="tpu_custom_call" | custom-call | flops 4000000000 | bytes 12320768 | tf_op jit(solution)/shard_map/pallas_call | solution.py:414
  218.7 8.1 %collective-permute-done.34 = bf16[128,1408]{1,0:T(8,128)(2,1)} collective-permute-done((bf16[128,1408]{1,0:T(8,128)(2,1)}, bf16[128,1408]{1,0:T(8,128)(2,1)}, u32[]{:S(2)}, u32[]{:S(2)}) %collective-permute-start.34) | collective-permute-done | bytes 360480 | tf_op jit(solution)/shard_map/ppermute | solution.py:442
  238.0 4.6 %collective-permute-done.24 = bf16[128,1280]{1,0:T(8,128)(2,1)S(1)} collective-permute-done((bf16[128,1280]{1,0:T(8,128)(2,1)}, bf16[128,1280]{1,0:T(8,128)(2,1)S(1)}, u32[]{:S(2)}, u32[]{:S(2)}) %collective-permute-start.24) | collective-permute-done | bytes 327712 | tf_op jit(solution)/shard_map/ppermute | solution.py:428
  246.0 5.8 %collective-permute-done.37.refs_1_ = bf16[128,1280]{1,0:T(8,128)(2,1)S(1)} collective-permute-done((bf16[128,1280]{1,0:T(8,128)(2,1)S(1)}, bf16[128,1280]{1,0:T(8,128)(2,1)S(1)}, u32[]{:S(2)}, u32[]{:S(2)}) %collective-permute-start.37) | collective-permute-done | bytes 327712 | tf_op jit(solution)/shard_map/ppermute | solution.py:442
  254.4 10.6 %shard_map.190 = (bf16[320,640]{1,0:T(8,128)(2,1)S(1)}, bf16[320,640]{1,0:T(8,128)(2,1)S(1)}, bf16[320,640]{1,0:T(8,128)(2,1)}, bf16[320,640]{1,0:T(8,128)(2,1)}...) custom-call(s32[48]{0:T(128)S(1)} %stack.107.info, ...), custom_call_target="tpu_custom_call" | custom-call | flops 5000000000 | bytes 14062592 | tf_op jit(solution)/shard_map/pallas_call | solution.py:414
  265.1 7.0 %shard_map.191 = (bf16[320,512]{1,0:T(8,128)(2,1)S(1)}, bf16[320,512]{1,0:T(8,128)(2,1)S(1)}, bf16[320,512]{1,0:T(8,128)(2,1)S(1)}, bf16[320,512]{1,0:T(8,128)(2,1)S(1)}, bf16[1024,384]{1,0:T(8,128)(2,1)}) custom-call(s32[48]{0:T(128)S(1)} %stack.107.info, bf16[1024,128]{1,0:T(8,128)(2,1)S(1)} %get-tuple-element.85.refs_0_, bf16[1024,256]{1,0:T(8,128)(2,1)S(1)} %copy-done.9, ...), custom_call_target="tpu_custom_call" | custom-call | flops 3000000000 | bytes 11113472 | tf_op jit(solution)/shard_map/pallas_call | solution.py:414
  284.3 4.9 %collective-permute-done.54 = bf16[320,512]{1,0:T(8,128)(2,1)S(1)} collective-permute-done((bf16[320,512]{1,0:T(8,128)(2,1)S(1)}, bf16[320,512]{1,0:T(8,128)(2,1)S(1)}, u32[]{:S(2)}, u32[]{:S(2)}) %collective-permute-start.54) | collective-permute-done | bytes 327712 | tf_op jit(solution)/shard_map/ppermute | solution.py:451
  291.9 4.2 %collective-permute-start.62 = (bf16[128,1280]{1,0:T(8,128)(2,1)}, bf16[128,1280]{1,0:T(8,128)(2,1)S(1)}, u32[]{:S(2)}, u32[]{:S(2)}) collective-permute-start(bf16[128,1280]{1,0:T(8,128)(2,1)} %get-tuple-element.161), channel_id=1, source_target_pairs={{0,3},{1,0},{2,1},{3,2},{4,11},{5,8},{6,9},{7,10},{8,7},{9,4},{10,... | collective-permute-start | bytes 983048 | tf_op jit(solution)/shard_map/ppermute | solution.py:502
  296.1 5.0 %collective-permute-done.52 = bf16[320,512]{1,0:T(8,128)(2,1)S(1)} collective-permute-done((bf16[320,512]{1,0:T(8,128)(2,1)S(1)}, bf16[320,512]{1,0:T(8,128)(2,1)S(1)}, u32[]{:S(2)}, u32[]{:S(2)}) %collective-permute-start.52) | collective-permute-done | bytes 327712 | tf_op jit(solution)/shard_map/ppermute | solution.py:451
  322.4 5.7 %all-to-all-start.1 = ((bf16[8,10,1152]{2,1,0:T(8,128)(2,1)}), bf16[8,10,1152]{2,1,0:T(8,128)(2,1)S(1)}, u32[]{:S(2)}, u32[]{:S(2)}) async-start(bf16[8,10,1152]{2,1,0:T(8,128)(2,1)} %reshape.94), calls=%async_computation.1 | async-start | bytes 589824 | tf_op jit(solution)/shard_map/all_to_all | solution.py:766
  (264 shorter events, 141.5 us)
Async XLA Ops:
  7.2 65.5 %all-gather.3.cloned.1.call-start = ((), (), s32[]{:S(2)}) async-start(), calls=%async_computation.3 | async-start | bytes 3133440 | tf_op jit(solution)/shard_map/all_gather | solution.py:567
  25.1 112.8 %all-gather.5.cloned.1.call-start = ((), (), s32[]{:S(2)}) async-start(), calls=%async_computation.4 | async-start | bytes 4177920 | tf_op jit(solution)/shard_map/all_gather | solution.py:578
  39.2 18.8 %collective-permute-start.18 = (bf16[80,1536]{1,0:T(8,128)(2,1)}, bf16[80,1536]{1,0:T(8,128)(2,1)S(1)}, u32[]{:S(2)}, u32[]{:S(2)}) collective-permute-start(bf16[80,1536]{1,0:T(8,128)(2,1)} %pad_maximum_fusion.3), channel_id=1, source_target_pairs={{0,0},{4,8},{8,16},{12,24},{16,4},{20,12},{24,20},{28,28},{1,1},{5... | collective-permute-start | bytes 737288 | tf_op jit(solution)/shard_map/ppermute | solution.py:433
  72.8 255.8 %reduce-scatter.2.cloned.1.call-start = ((), (), s32[]{:S(2)}) async-start(), calls=%async_computation.5 | async-start | bytes 4177920 | tf_op jit(solution)/shard_map/reduce_scatter | solution.py:665
  99.2 17.9 %collective-permute-start.9 = (bf16[128,1280]{1,0:T(8,128)(2,1)S(1)}, bf16[128,1280]{1,0:T(8,128)(2,1)S(1)}, u32[]{:S(2)}, u32[]{:S(2)}) collective-permute-start(bf16[128,1280]{1,0:T(8,128)(2,1)S(1)} %get-tuple-element.168), channel_id=1, source_target_pairs={{0,1},{1,2},{2,3},{3,0},{4,5},{5,6},{6,7},{7,4},{8,9},{9,10},{10,1... | collective-permute-start | bytes 983048 | tf_op jit(solution)/shard_map/ppermute | solution.py:442
  119.4 17.2 %collective-permute-start.12 = (bf16[128,1280]{1,0:T(8,128)(2,1)S(1)}, bf16[128,1280]{1,0:T(8,128)(2,1)S(1)}, u32[]{:S(2)}, u32[]{:S(2)}) collective-permute-start(bf16[128,1280]{1,0:T(8,128)(2,1)S(1)} %multiply_convert_fusion.refs_0_), channel_id=1, source_target_pairs={{0,1},{1,2},{2,3},{3,0},{4,5},{5,6},{6,7},{7,4},{8,9},{9,10},{10,1... | collective-permute-start | bytes 983048 | tf_op jit(solution)/shard_map/ppermute | solution.py:442
  119.5 18.3 %collective-permute-start.13 = (bf16[128,1280]{1,0:T(8,128)(2,1)S(1)}, bf16[128,1280]{1,0:T(8,128)(2,1)S(1)}, u32[]{:S(2)}, u32[]{:S(2)}) collective-permute-start(bf16[128,1280]{1,0:T(8,128)(2,1)S(1)} %multiply_convert_fusion.refs_0_), channel_id=1, source_target_pairs={{0,2},{1,3},{2,0},{3,1},{4,6},{5,7},{6,4},{7,5},{8,10},{9,11},{10,... | collective-permute-start | bytes 983048 | tf_op jit(solution)/shard_map/ppermute | solution.py:442
  120.0 17.9 %collective-permute-start.14 = (bf16[128,1280]{1,0:T(8,128)(2,1)S(1)}, bf16[128,1280]{1,0:T(8,128)(2,1)S(1)}, u32[]{:S(2)}, u32[]{:S(2)}) collective-permute-start(bf16[128,1280]{1,0:T(8,128)(2,1)S(1)} %multiply_convert_fusion.refs_0_), channel_id=1, source_target_pairs={{0,3},{1,0},{2,1},{3,2},{4,7},{5,4},{6,5},{7,6},{8,11},{9,8},{10,9... | collective-permute-start | bytes 983048 | tf_op jit(solution)/shard_map/ppermute | solution.py:442
  122.2 16.7 %collective-permute-start.15 = (bf16[128,1280]{1,0:T(8,128)(2,1)S(1)}, bf16[128,1280]{1,0:T(8,128)(2,1)S(1)}, u32[]{:S(2)}, u32[]{:S(2)}) collective-permute-start(bf16[128,1280]{1,0:T(8,128)(2,1)S(1)} %multiply_convert_fusion.refs_0_), channel_id=1, source_target_pairs={{0,8},{8,0},{1,9},{9,1},{2,10},{10,2},{3,11},{11,3},{4,12},{12,4},... | collective-permute-start | bytes 983048 | tf_op jit(solution)/shard_map/ppermute | solution.py:466
  155.4 17.7 %collective-permute-start.21 = (bf16[128,1280]{1,0:T(8,128)(2,1)S(1)}, bf16[128,1280]{1,0:T(8,128)(2,1)S(1)}, u32[]{:S(2)}, u32[]{:S(2)}) collective-permute-start(bf16[128,1280]{1,0:T(8,128)(2,1)S(1)} %get-tuple-element.165), channel_id=1, source_target_pairs={{0,1},{1,2},{2,3},{3,0},{4,5},{5,6},{6,7},{7,4},{8,9},{9,10},{10,1... | collective-permute-start | bytes 983048 | tf_op jit(solution)/shard_map/ppermute | solution.py:442
  174.2 18.3 %collective-permute-start.27 = (bf16[128,1280]{1,0:T(8,128)(2,1)S(1)}, bf16[128,1280]{1,0:T(8,128)(2,1)S(1)}, u32[]{:S(2)}, u32[]{:S(2)}) collective-permute-start(bf16[128,1280]{1,0:T(8,128)(2,1)S(1)} %fusion.11.refs_0_), channel_id=1, source_target_pairs={{0,2},{1,3},{2,0},{3,1},{4,6},{5,7},{6,4},{7,5},{8,10},{9,11},{10,... | collective-permute-start | bytes 983048 | tf_op jit(solution)/shard_map/ppermute | solution.py:442
  175.9 16.7 %collective-permute-start.28 = (bf16[128,1280]{1,0:T(8,128)(2,1)S(1)}, bf16[128,1280]{1,0:T(8,128)(2,1)S(1)}, u32[]{:S(2)}, u32[]{:S(2)}) collective-permute-start(bf16[128,1280]{1,0:T(8,128)(2,1)S(1)} %fusion.11.refs_0_), channel_id=1, source_target_pairs={{0,3},{1,0},{2,1},{3,2},{4,7},{5,4},{6,5},{7,6},{8,11},{9,8},{10,9... | collective-permute-start | bytes 983048 | tf_op jit(solution)/shard_map/ppermute | solution.py:442
  176.8 16.5 %collective-permute-start.29 = (bf16[128,1280]{1,0:T(8,128)(2,1)S(1)}, bf16[128,1280]{1,0:T(8,128)(2,1)S(1)}, u32[]{:S(2)}, u32[]{:S(2)}) collective-permute-start(bf16[128,1280]{1,0:T(8,128)(2,1)S(1)} %fusion.11.refs_0_), channel_id=1, source_target_pairs={{0,8},{8,0},{1,9},{9,1},{2,10},{10,2},{3,11},{11,3},{4,12},{12,4},... | collective-permute-start | bytes 983048 | tf_op jit(solution)/shard_map/ppermute | solution.py:466
  207.5 19.3 %collective-permute-start.34 = (bf16[128,1408]{1,0:T(8,128)(2,1)}, bf16[128,1408]{1,0:T(8,128)(2,1)}, u32[]{:S(2)}, u32[]{:S(2)}) collective-permute-start(bf16[128,1408]{1,0:T(8,128)(2,1)} %get-tuple-element.158), channel_id=1, source_target_pairs={{0,1},{1,2},{2,3},{3,0},{4,5},{5,6},{6,7},{7,4},{8,9},{9,10},{10,1... | collective-permute-start | bytes 1081352 | tf_op jit(solution)/shard_map/ppermute | solution.py:442
  234.1 17.7 %collective-permute-start.37 = (bf16[128,1280]{1,0:T(8,128)(2,1)S(1)}, bf16[128,1280]{1,0:T(8,128)(2,1)S(1)}, u32[]{:S(2)}, u32[]{:S(2)}) collective-permute-start(bf16[128,1280]{1,0:T(8,128)(2,1)S(1)} %get-tuple-element.171.refs_0_), channel_id=1, source_target_pairs={{0,1},{1,2},{2,3},{3,0},{4,5},{5,6},{6,7},{7,4},{8,9},{9,10},{10,1... | collective-permute-start | bytes 983048 | tf_op jit(solution)/shard_map/ppermute | solution.py:442
  234.2 17.7 %collective-permute-start.38 = (bf16[128,1280]{1,0:T(8,128)(2,1)S(1)}, bf16[128,1280]{1,0:T(8,128)(2,1)S(1)}, u32[]{:S(2)}, u32[]{:S(2)}) collective-permute-start(bf16[128,1280]{1,0:T(8,128)(2,1)S(1)} %get-tuple-element.171.refs_0_), channel_id=1, source_target_pairs={{0,2},{1,3},{2,0},{3,1},{4,6},{5,7},{6,4},{7,5},{8,10},{9,11},{10,... | collective-permute-start | bytes 983048 | tf_op jit(solution)/shard_map/ppermute | solution.py:442
  236.1 16.6 %collective-permute-start.39 = (bf16[128,1280]{1,0:T(8,128)(2,1)S(1)}, bf16[128,1280]{1,0:T(8,128)(2,1)S(1)}, u32[]{:S(2)}, u32[]{:S(2)}) collective-permute-start(bf16[128,1280]{1,0:T(8,128)(2,1)S(1)} %get-tuple-element.171.refs_0_), channel_id=1, source_target_pairs={{0,3},{1,0},{2,1},{3,2},{4,7},{5,4},{6,5},{7,6},{8,11},{9,8},{10,9... | collective-permute-start | bytes 983048 | tf_op jit(solution)/shard_map/ppermute | solution.py:442
  237.6 16.7 %collective-permute-start.40 = (bf16[128,1280]{1,0:T(8,128)(2,1)S(1)}, bf16[128,1280]{1,0:T(8,128)(2,1)S(1)}, u32[]{:S(2)}, u32[]{:S(2)}) collective-permute-start(bf16[128,1280]{1,0:T(8,128)(2,1)S(1)} %get-tuple-element.171.refs_0_), channel_id=1, source_target_pairs={{0,8},{8,0},{1,9},{9,1},{2,10},{10,2},{3,11},{11,3},{4,12},{12,4},... | collective-permute-start | bytes 983048 | tf_op jit(solution)/shard_map/ppermute | solution.py:466
  281.1 20.0 %collective-permute-start.52 = (bf16[320,512]{1,0:T(8,128)(2,1)S(1)}, bf16[320,512]{1,0:T(8,128)(2,1)S(1)}, u32[]{:S(2)}, u32[]{:S(2)}) collective-permute-start(bf16[320,512]{1,0:T(8,128)(2,1)S(1)} %get-tuple-element.96), channel_id=1, source_target_pairs={{0,16},{16,4},{4,20},{20,0},{1,17},{17,5},{5,21},{21,1},{2,18},{18... | collective-permute-start | bytes 983048 | tf_op jit(solution)/shard_map/ppermute | solution.py:451
  281.1 24.1 %collective-permute-start.48 = (bf16[320,640]{1,0:T(8,128)(2,1)S(1)}, bf16[320,640]{1,0:T(8,128)(2,1)S(1)}, u32[]{:S(2)}, u32[]{:S(2)}) collective-permute-start(bf16[320,640]{1,0:T(8,128)(2,1)S(1)} %copy-done.30), channel_id=1, source_target_pairs={{0,96},{32,0},{64,32},{96,64},{1,97},{33,1},{65,33},{97,65},{2,98}... | collective-permute-start | bytes 1228808 | tf_op jit(solution)/shard_map/ppermute | solution.py:446
  281.6 24.3 %collective-permute-start.47 = (bf16[320,640]{1,0:T(8,128)(2,1)S(1)}, bf16[320,640]{1,0:T(8,128)(2,1)S(1)}, u32[]{:S(2)}, u32[]{:S(2)}) collective-permute-start(bf16[320,640]{1,0:T(8,128)(2,1)S(1)} %copy-done.29), channel_id=1, source_target_pairs={{0,64},{32,96},{64,0},{96,32},{1,65},{33,97},{65,1},{97,33},{2,66}... | collective-permute-start | bytes 1228808 | tf_op jit(solution)/shard_map/ppermute | solution.py:446
  289.2 18.2 %collective-permute-start.46 = (bf16[320,640]{1,0:T(8,128)(2,1)S(1)}, bf16[320,640]{1,0:T(8,128)(2,1)S(1)}, u32[]{:S(2)}, u32[]{:S(2)}) collective-permute-start(bf16[320,640]{1,0:T(8,128)(2,1)S(1)} %get-tuple-element.91), channel_id=1, source_target_pairs={{0,32},{32,64},{64,96},{96,0},{1,33},{33,65},{65,97},{97,1},{2,34}... | collective-permute-start | bytes 1228808 | tf_op jit(solution)/shard_map/ppermute | solution.py:446
  291.9 36.2 %collective-permute-start.62 = (bf16[128,1280]{1,0:T(8,128)(2,1)}, bf16[128,1280]{1,0:T(8,128)(2,1)S(1)}, u32[]{:S(2)}, u32[]{:S(2)}) collective-permute-start(bf16[128,1280]{1,0:T(8,128)(2,1)} %get-tuple-element.161), channel_id=1, source_target_pairs={{0,3},{1,0},{2,1},{3,2},{4,11},{5,8},{6,9},{7,10},{8,7},{9,4},{10,... | collective-permute-start | bytes 983048 | tf_op jit(solution)/shard_map/ppermute | solution.py:502
  301.1 27.0 %collective-permute-start.61 = (bf16[128,1280]{1,0:T(8,128)(2,1)}, bf16[128,1280]{1,0:T(8,128)(2,1)S(1)}, u32[]{:S(2)}, u32[]{:S(2)}) collective-permute-start(bf16[128,1280]{1,0:T(8,128)(2,1)} %get-tuple-element.162), channel_id=1, source_target_pairs={{0,2},{1,3},{2,0},{3,1},{4,10},{5,11},{6,8},{7,9},{8,6},{9,7},{10,... | collective-permute-start | bytes 983048 | tf_op jit(solution)/shard_map/ppermute | solution.py:502
  (76 other events, 664.3 us)
Sparse Core Ops, SparseCore 0:
  25.2 47.4 all-gather.2
  75.4 49.7 all-gather.4
  215.8 85.1 reduce-scatter.1
